TPU v7x, 32 devices: a whole 2x2x4 slice. The times are simulated.
32 devices in a mesh: groups: 2 (over y), aux: 4 (over x, core), pair: 4 (over z).
Axes of the slice: x: 2, y: 2, z: 4, core: 2. Of those that a mesh axis runs over, the one named last changes fastest.
Arguments:
- tile_values: bfloat16 [256, 64, 4096], P('pair', ('groups', 'aux')), parts along dimension 1, may hold values from -6 to 6
- tile_pairs: int32 [256, 2], P('pair'), may hold values from 0 to 319, as said below
- tile_counts: int32 [4], P('pair'), may hold values from 8 to 64, as said below
- coeffs: bfloat16 [20480, 32], P('pair', 'groups'), parts along dimension 1, may hold values from -0.25 to 0.25
- domains: int32 [32, 8], P('groups'), parts along dimension 0, may hold values from 0 to 319, as said below
- virtual: bfloat16 [32, 512, 256], P(('groups', 'pair', 'aux')), parts along dimension 0, may hold values from -0.25 to 0.25
Outputs:
- fitted: bfloat16 [16, 64, 256], P(('pair', 'aux'), 'groups'), parts along dimension 1
There are 2 independent parts, one for each index of `groups`. A program takes and returns all parts, laid end to end along the dimension named above; an argument that names none is the same for every part. Nothing has to cross between parts.
Inputs may be any that keep to these rules, and one draw needn't show every extreme that they name: `tile_pairs`: the list of pair device p holds distinct pairs; every slot, live or not, has its mu block among that device's own blocks p * 80 to p * 80 + 79, and its nu block within 3 blocks of the mu block, cyclically modulo 320. Slots from the device's tile_counts entry on are padding. `tile_counts`: some device's list is full in every draw. `domains`: the domain of orbital i, listed in some order, is the cyclic run of 8 consecutive blocks modulo 320 that begins at a block from p * 80 to p * 80 + 79, where p = floor(i * 320 / 1280).
All inputs are finite; a program needn't handle non-finite values.
Results may differ from a plain program's by a relative error of at most 0.0051.
Values may be sent and summed in bfloat16 or wider, within the bound.
No kernel may reach another device: no remote copies, remote signals or barrier semaphores. Data moves between devices by JAX's collectives and lax.ppermute only.
A program may use at most 64 MiB of HBM per device.

v0:
```python
import functools

import jax
import jax.numpy as jnp
from jax import lax
from jax.experimental import pallas as pl
from jax.experimental.pallas import tpu as pltpu
from jax.sharding import PartitionSpec as P

BLOCK = 64
LANES = 128
WORD = 32
UNROLL = 2
EARLY = 16


def half_kernel(sizes, count_s, pairs_hbm, dom_hbm, coef_hbm, tiles_hbm,
                own, prior,
                pairs_v, dom_s, coef_v, coef_f, tiles_v, hits_v, hits_s, found, todo,
                masks, picked, weights, sums, sems):
    slots, aux_dev, slab, domain_len, own_blocks, pair_size = sizes
    pair_id = lax.axis_index("pair")
    aux_id = lax.axis_index("aux")
    first_block = pair_id * own_blocks
    own_row = pair_id * slab
    prior_row = lax.rem(pair_id + pair_size - 1, pair_size) * slab
    half_rows = BLOCK // 2
    orbitals = 2 * slab

    small = [
        pltpu.make_async_copy(dom_hbm, dom_s, sems.at[0]),
        pltpu.make_async_copy(pairs_hbm, pairs_v, sems.at[1]),
        pltpu.make_async_copy(coef_hbm, coef_v, sems.at[2]),
    ]
    for copy in small:
        copy.start()
    early = pltpu.make_async_copy(
        tiles_hbm.at[pl.ds(0, EARLY)], tiles_v.at[pl.ds(0, EARLY)], sems.at[3])
    early.start()

    row_i = lax.broadcasted_iota(jnp.int32, (half_rows, LANES), 0)
    lane_i = lax.broadcasted_iota(jnp.int32, (half_rows, LANES), 1)
    for e in range(2):
        masks[e] = (lax.shift_right_arithmetic(lane_i - e * BLOCK, 1) == row_i).astype(jnp.float32)
    src = lax.broadcasted_iota(jnp.int32, (LANES, LANES), 0)
    dst = lax.broadcasted_iota(jnp.int32, (LANES, LANES), 1)
    spread = ((src & 1) == lax.shift_right_logical(dst, 6)).astype(jnp.bfloat16)
    sums[...] = jnp.zeros_like(sums)
    weights[pl.ds(orbitals * domain_len * half_rows, half_rows), :] = jnp.zeros((half_rows, LANES), jnp.float32)

    for copy in small[:2]:
        copy.wait()

    def orbital_row(i):
        return own_row + i if i < slab else prior_row + i - slab

    slot_i = lax.broadcasted_iota(jnp.int32, (1, slots), 1)
    live = slot_i < count_s[0]
    mu = pairs_v[0:1, :]
    nu = pairs_v[1:2, :]
    taken = jnp.zeros((1, slots), jnp.int32)
    coded = [jnp.zeros((1, slots), jnp.int32) for _ in range(orbitals)]
    for i in range(orbitals):
        row = orbital_row(i)
        at_mu = jnp.full((1, slots), -1, jnp.int32)
        at_nu = jnp.full((1, slots), -1, jnp.int32)
        for s in range(domain_len):
            block = dom_s[s, row]
            at_mu = jnp.where(mu == block, s, at_mu)
            at_nu = jnp.where(nu == block, s, at_nu)
        hit = live & (at_mu >= 0) & (at_nu >= 0)
        code = (i * domain_len + at_mu) * domain_len + at_nu
        for k in range(i + 1):
            coded[k] = jnp.where(hit & (taken == k), code, coded[k])
        taken = taken + hit.astype(jnp.int32)
    for k in range(orbitals):
        hits_v[k:k + 1, 0:slots] = coded[k]
    hits_v[orbitals:orbitals + 1, 0:slots] = taken
    hits_copy = pltpu.make_async_copy(hits_v, hits_s, sems.at[0])
    hits_copy.start()

    number = jnp.int32(0)
    early_number = number
    for first in range(0, slots, WORD):
        inside = (taken > 0) & (slot_i >= first) & (slot_i < first + WORD)
        word = jnp.sum(jnp.where(inside, lax.shift_left(1, slot_i & (WORD - 1)), 0))
        for t in range(WORD):
            if first + t == EARLY:
                early_number = number
            found[number] = first + t
            number = number + (lax.shift_right_logical(word, t) & 1)

    def tile_copy(t):
        return pltpu.make_async_copy(tiles_hbm.at[t], tiles_v.at[t], sems.at[4])

    @pl.loop(early_number, number)
    def _(j):
        tile_copy(found[j]).start()

    small[2].wait()
    for e in range(own_blocks // 2):
        coef_f[e] = coef_v[:, e * LANES:(e + 1) * LANES].astype(jnp.float32)

    for i in range(orbitals):
        row = orbital_row(i)
        for s in range(domain_len):
            local = jnp.clip(dom_s[s, row] - first_block, 0, own_blocks - 1)
            line = coef_f[lax.shift_right_logical(local, 1), pl.ds(row, 1), :]
            picked[pl.ds(s * half_rows, half_rows), :] = (masks[local & 1] * line).astype(jnp.bfloat16)
        weights[pl.ds(i * domain_len * half_rows, domain_len * half_rows), :] = jnp.dot(
            picked[...], spread, preferred_element_type=jnp.float32)

    hits_copy.wait()

    def listed(j, filled):
        t = found[j]

        def entry(k, at):
            todo[at] = hits_s[k, t] * slots + t
            return at + 1

        return lax.fori_loop(0, hits_s[orbitals, t], entry, filled)

    nothing = orbitals * domain_len * domain_len * slots
    early_hits = lax.fori_loop(0, early_number, listed, jnp.int32(0))
    for u in range(UNROLL - 1):
        todo[early_hits + u] = nothing
    early_steps = lax.div(early_hits + UNROLL - 1, UNROLL)
    hits = lax.fori_loop(early_number, number, listed, early_steps * UNROLL)
    for u in range(UNROLL - 1):
        todo[hits + u] = nothing
    steps = lax.div(hits + UNROLL - 1, UNROLL)

    def work(step):
        totals = []
        for u in range(UNROLL):
            word = todo[step * UNROLL + u]
            t = word & (slots - 1)
            code = lax.div(word, slots)
            at_nu = lax.rem(code, domain_len)
            source = lax.div(code, domain_len)
            base = source * half_rows
            target = lax.div(source, domain_len) * domain_len + at_nu
            parts = [None] * 4
            for h in range(half_rows):
                term = (tiles_v[t, :, h * LANES:(h + 1) * LANES].astype(jnp.float32)
                        * weights[pl.ds(base + h, 1), :])
                parts[h % 4] = term if parts[h % 4] is None else parts[h % 4] + term
            totals.append((target, (parts[0] + parts[1]) + (parts[2] + parts[3])))
        for target, total in totals:
            sums[target] += total

    early.wait()
    pl.loop(0, early_steps)(work)

    @pl.loop(early_number, number)
    def _(j):
        tile_copy(found[j]).wait()

    pl.loop(early_steps, steps)(work)

    low = lax.broadcasted_iota(jnp.int32, (aux_dev, LANES), 1) < BLOCK

    def folded(i, u):
        left = sums[i * domain_len + 2 * u]
        right = sums[i * domain_len + 2 * u + 1]
        return jnp.where(low, left + pltpu.roll(left, BLOCK, 1), right + pltpu.roll(right, BLOCK, 1))

    for r in range(slab):
        target = lax.bitwise_xor(aux_id, r)
        for first, out in ((0, own), (slab, prior)):
            for u in range(domain_len // 2):
                out[r, :, u * LANES:(u + 1) * LANES] = folded(first + target, u)


def half_blocks(tile_values, tile_pairs, tile_counts, coeffs, domains, slab, pair_size):
    slots, aux_dev, flat = tile_values.shape
    orbitals = coeffs.shape[1]
    domain_len = domains.shape[1]
    own_blocks = coeffs.shape[0] // BLOCK
    hits_rows = (2 * slab + 8) // 8 * 8
    sizes = (slots, aux_dev, slab, domain_len, own_blocks, pair_size)
    out = jax.ShapeDtypeStruct((slab, aux_dev, domain_len * BLOCK), jnp.float32)
    any_spec = pl.BlockSpec(memory_space=pltpu.HBM)
    return pl.pallas_call(
        functools.partial(half_kernel, sizes),
        out_shape=[out] * 2,
        in_specs=[pl.BlockSpec(memory_space=pltpu.SMEM)] + [any_spec] * 4,
        out_specs=[pl.BlockSpec(memory_space=pltpu.VMEM)] * 2,
        scratch_shapes=[
            pltpu.VMEM((2, slots), jnp.int32),
            pltpu.SMEM((domain_len, orbitals), jnp.int32),
            pltpu.VMEM((orbitals, own_blocks * BLOCK), jnp.bfloat16),
            pltpu.VMEM((own_blocks * BLOCK // LANES, orbitals, LANES), jnp.float32),
            pltpu.VMEM((slots, aux_dev, flat), jnp.bfloat16),
            pltpu.VMEM((hits_rows, LANES), jnp.int32),
            pltpu.SMEM((hits_rows, LANES), jnp.int32),
            pltpu.SMEM((slots + 1,), jnp.int32),
            pltpu.SMEM((2 * slab * slots + 2 * UNROLL,), jnp.int32),
            pltpu.VMEM((2, BLOCK // 2, LANES), jnp.float32),
            pltpu.VMEM((domain_len * BLOCK // 2, LANES), jnp.bfloat16),
            pltpu.VMEM(((2 * slab * domain_len + 1) * BLOCK // 2, LANES), jnp.float32),
            pltpu.VMEM((2 * slab * domain_len + 1, aux_dev, LANES), jnp.float32),
            pltpu.SemaphoreType.DMA((5,)),
        ],
        compiler_params=pltpu.CompilerParams(vmem_limit_bytes=32 * 1024 * 1024),
    )(tile_counts, *[pltpu.with_memory_space_constraint(value, pltpu.HBM)
                     for value in (tile_pairs.T, domains.T, coeffs.T, tile_values)])


def moved(value, aux_mask, pair_step):
    aux_size, pair_size = lax.axis_size("aux"), lax.axis_size("pair")
    routes = [
        (a * pair_size + p, (a ^ aux_mask) * pair_size + (p + pair_step) % pair_size)
        for a in range(aux_size)
        for p in range(pair_size)
    ]
    return lax.ppermute(value, ("aux", "pair"), routes)


def fit_kernel(sources, *refs):
    count = len(refs) - 3
    virtual, fitted, rows = refs[count:]
    aux_id = lax.axis_index("aux")
    height = refs[0].shape[1]
    for offset, ref, place in sources:
        start = pl.multiple_of(lax.bitwise_xor(aux_id, offset) * height, height)
        rows[pl.ds(start, height), :] = refs[ref][place].astype(jnp.float32)
    fitted[0] = jnp.dot(rows[...].astype(jnp.bfloat16), virtual[0],
                        preferred_element_type=jnp.float32).astype(fitted.dtype)


def body(tile_values, tile_pairs, tile_counts, coeffs, domains, virtual):
    pair_size = lax.axis_size("pair")
    aux_size = lax.axis_size("aux")
    slab = coeffs.shape[1] // pair_size
    aux_dev = tile_values.shape[1]
    own, prior = half_blocks(tile_values, tile_pairs, tile_counts, coeffs, domains, slab, pair_size)
    blocks = (own + moved(prior, 0, -1)).astype(jnp.bfloat16)

    items = [(blocks, 0, 0)]
    half = aux_size
    while half > 2:
        half //= 2
        mask = half | 1
        sent = moved(jnp.concatenate([value[half:] for value, _, _ in items]), mask, 0)
        kept = [(value[:half], flip, source) for value, flip, source in items]
        got = [(sent[k * half:(k + 1) * half], flip ^ 1, source ^ mask) for k, (_, flip, source) in enumerate(items)]
        items = kept + got
    last = moved(jnp.concatenate([value[1 - flip:2 - flip] for value, flip, _ in items]), 1, 0)
    sources = []
    for k, (_, flip, source) in enumerate(items):
        sources.append((source, k, flip))
        sources.append((source ^ 1, len(items), k))
    arrays = [item[0] for item in items] + [last]
    return pl.pallas_call(
        functools.partial(fit_kernel, sources),
        out_shape=jax.ShapeDtypeStruct((1, aux_size * aux_dev, virtual.shape[2]), jnp.bfloat16),
        in_specs=[pl.BlockSpec(memory_space=pltpu.VMEM)] * (len(arrays) + 1),
        out_specs=pl.BlockSpec(memory_space=pltpu.VMEM),
        scratch_shapes=[pltpu.VMEM((aux_size * aux_dev, virtual.shape[1]), jnp.float32)],
        compiler_params=pltpu.CompilerParams(vmem_limit_bytes=16 * 1024 * 1024),
    )(*arrays, virtual)


def solution(mesh):
    placed = (
        P("pair", ("groups", "aux"), None),
        P("pair", None),
        P("pair"),
        P("pair", "groups"),
        P("groups", None),
        P(("groups", "pair", "aux"), None, None),
    )
    return jax.shard_map(
        body,
        mesh=mesh,
        in_specs=placed,
        out_specs=P(("pair", "aux"), "groups", None),
        check_vma=False,
    )
```

profile of v0, /device:TPU:0, one launch (start us, length us, event | category | flops | bytes accessed | tf_op | source)
XLA Modules:
  0.0 15.3 jit_solution(7856124498496113440)
XLA Ops:
  0.0 0.0 copy-start
  0.7 3.0 %shard_map.64 = (f32[4,8,512]{2,1,0:T(8,128)S(1)}, f32[4,8,512]{2,1,0:T(8,128)S(1)}) custom-call(s32[1]{0:T(128)S(6)} %copy.7.count_s, s32[2,64]{1,0:T(2,128)} %bitcast.5, s32[8,16]{1,0:T(8,128)} %bitcast.4, bf16[16,5120]{1,0:T(8,128)(2,1)} %bitcast.3, bf16[64,8,4096]{2,1,0:T(8,128)(2,1)} %tiles_hbm.1), custom_call_target="tpu_custom_call" | custom-call | tf_op jit(solution)/shard_map/pallas_call | solution.py:185
  3.7 4.4 %collective-permute-start = (f32[4,8,512]{2,1,0:T(8,128)S(1)}, f32[4,8,512]{2,1,0:T(8,128)S(1)}, u32[]{:S(2)}, u32[]{:S(2)}) collective-permute-start(f32[4,8,512]{2,1,0:T(8,128)S(1)} %get-tuple-element.8), channel_id=1, source_target_pairs={{0,3},{1,0},{2,1},{3,2},{4,7},{5,4},{6,5},{7,6},{8,11},{9,8},{10,9... | collective-permute-start | bytes 196616 | tf_op jit(solution)/shard_map/ppermute | solution.py:218
  8.1 1.9 %collective-permute-done = f32[4,8,512]{2,1,0:T(8,128)S(1)} collective-permute-done((f32[4,8,512]{2,1,0:T(8,128)S(1)}, f32[4,8,512]{2,1,0:T(8,128)S(1)}, u32[]{:S(2)}, u32[]{:S(2)}) %collective-permute-start) | collective-permute-done | bytes 65568 | tf_op jit(solution)/shard_map/ppermute | solution.py:218
  10.0 0.1 collective-permute-start.1
  10.2 3.2 %collective-permute-done.1.refs_1_ = bf16[2,8,512]{2,1,0:T(8,128)(2,1)S(1)} collective-permute-done((bf16[2,8,512]{2,1,0:T(8,128)(2,1)S(1)}, bf16[2,8,512]{2,1,0:T(8,128)(2,1)S(1)}, u32[]{:S(2)}, u32[]{:S(2)}) %collective-permute-start.1) | collective-permute-done | bytes 16416 | tf_op jit(solution)/shard_map/ppermute | solution.py:218
  13.4 0.1 collective-permute-start.2
  13.5 1.1 %collective-permute-done.2.refs_2_ = bf16[2,8,512]{2,1,0:T(8,128)(2,1)S(1)} collective-permute-done((bf16[2,8,512]{2,1,0:T(8,128)(2,1)S(1)}, bf16[2,8,512]{2,1,0:T(8,128)(2,1)S(1)}, u32[]{:S(2)}, u32[]{:S(2)}) %collective-permute-start.2) | collective-permute-done | bytes 16416 | tf_op jit(solution)/shard_map/ppermute | solution.py:218
  14.6 0.0 copy-done
  14.6 0.8 %shard_map.65 = bf16[1,32,256]{2,1,0:T(8,128)(2,1)} custom-call(bf16[2,8,512]{2,1,0:T(8,128)(2,1)S(1)} %get-tuple-element.10.refs_0_, bf16[2,8,512]{2,1,0:T(8,128)(2,1)S(1)} %collective-permute-done.1.refs_1_, bf16[2,8,512]{2,1,0:T(8,128)(2,1)S(1)} %collective-permute-done.2.refs_2_, bf16[1,512,256]{2,1,0:T(8,128)(2,1)S(1)} %copy-done), custom_call_target="tpu_custom_call" | custom-call | tf_op jit(solution)/shard_map/pallas_call | solution.py:256
  (5 shorter events, 0.0 us)
Async XLA Ops:
  0.0 14.6 %copy-start = (bf16[1,512,256]{2,1,0:T(8,128)(2,1)S(1)}, bf16[1,512,256]{2,1,0:T(8,128)(2,1)}, u32[]{:S(2)}) copy-start(bf16[1,512,256]{2,1,0:T(8,128)(2,1)} %refs_3_.1) | copy-start | bytes 786436
  3.7 6.3 %collective-permute-start = (f32[4,8,512]{2,1,0:T(8,128)S(1)}, f32[4,8,512]{2,1,0:T(8,128)S(1)}, u32[]{:S(2)}, u32[]{:S(2)}) collective-permute-start(f32[4,8,512]{2,1,0:T(8,128)S(1)} %get-tuple-element.8), channel_id=1, source_target_pairs={{0,3},{1,0},{2,1},{3,2},{4,7},{5,4},{6,5},{7,6},{8,11},{9,8},{10,9... | collective-permute-start | bytes 196616 | tf_op jit(solution)/shard_map/ppermute | solution.py:218
  10.0 3.4 %collective-permute-start.1 = (bf16[2,8,512]{2,1,0:T(8,128)(2,1)S(1)}, bf16[2,8,512]{2,1,0:T(8,128)(2,1)S(1)}, u32[]{:S(2)}, u32[]{:S(2)}) collective-permute-start(bf16[2,8,512]{2,1,0:T(8,128)(2,1)S(1)} %get-tuple-element.9), channel_id=1, source_target_pairs={{0,12},{1,13},{2,14},{3,15},{4,8},{5,9},{6,10},{7,11},{8,4},{9,5},... | collective-permute-start | bytes 49160 | tf_op jit(solution)/shard_map/ppermute | solution.py:218
  13.4 1.2 %collective-permute-start.2 = (bf16[2,8,512]{2,1,0:T(8,128)(2,1)S(1)}, bf16[2,8,512]{2,1,0:T(8,128)(2,1)S(1)}, u32[]{:S(2)}, u32[]{:S(2)}) collective-permute-start(bf16[2,8,512]{2,1,0:T(8,128)(2,1)S(1)} %pad_maximum_fusion), channel_id=1, source_target_pairs={{0,4},{1,5},{2,6},{3,7},{4,0},{5,1},{6,2},{7,3},{8,12},{9,13},{10,... | collective-permute-start | bytes 49160 | tf_op jit(solution)/shard_map/ppermute | solution.py:218
where the time goes:
time: 15.5 us; the launch traced here: 15.3 us
  waiting for transfers between devices  6.19 us (40%)
  starting transfers between devices  4.63 us (30%)
  Pallas kernels  3.77 us (24%)
  between operations  0.72 us (5%)
    ppermute x3, waiting for transfers between devices, moved(): return lax.ppermute(value, ('aux', 'pair'), routes)  6.19 us
    ppermute x3, starting transfers between devices, moved(): return lax.ppermute(value, ('aux', 'pair'), routes)  4.63 us
    pallas_call x1, Pallas kernels, half_blocks(): pl.pallas_call(functools.partial(half_kernel, sizes), out_shape=[out] * 2...  3.01 us
    pallas_call x1, Pallas kernels, body(): pl.pallas_call(functools.partial(fit_kernel, sources), out_shape=jax.Shap...  0.76 us
  transfers between devices with their start and end apart: 3, of which 3 were waited for; matrix products, arithmetic and copies ran while one was open for 0% of the time, Pallas kernels for 0%

commit v1 on v0

--- a/solution.py
+++ b/solution.py
@@ -11,11 +11,12 @@
 LANES = 128
 WORD = 32
 UNROLL = 2
-EARLY = 16
+EARLY = 32
+CHUNK = 4
 
 
 def half_kernel(sizes, count_s, pairs_hbm, dom_hbm, coef_hbm, tiles_hbm,
-                own, prior,
+                own_keep, own_send, prior_keep, prior_send,
                 pairs_v, dom_s, coef_v, coef_f, tiles_v, hits_v, hits_s, found, todo,
                 masks, picked, weights, sums, sems):
     slots, aux_dev, slab, domain_len, own_blocks, pair_size = sizes
@@ -34,9 +35,9 @@
     ]
     for copy in small:
         copy.start()
-    early = pltpu.make_async_copy(
-        tiles_hbm.at[pl.ds(0, EARLY)], tiles_v.at[pl.ds(0, EARLY)], sems.at[3])
-    early.start()
+    for first in range(0, EARLY, CHUNK):
+        pltpu.make_async_copy(
+            tiles_hbm.at[pl.ds(first, CHUNK)], tiles_v.at[pl.ds(first, CHUNK)], sems.at[3]).start()
 
     row_i = lax.broadcasted_iota(jnp.int32, (half_rows, LANES), 0)
     lane_i = lax.broadcasted_iota(jnp.int32, (half_rows, LANES), 1)
@@ -150,7 +151,7 @@
         for target, total in totals:
             sums[target] += total
 
-    early.wait()
+    pltpu.make_async_copy(tiles_hbm.at[pl.ds(0, EARLY)], tiles_v.at[pl.ds(0, EARLY)], sems.at[3]).wait()
     pl.loop(0, early_steps)(work)
 
     @pl.loop(early_number, number)
@@ -159,18 +160,20 @@
 
     pl.loop(early_steps, steps)(work)
 
-    low = lax.broadcasted_iota(jnp.int32, (aux_dev, LANES), 1) < BLOCK
-
-    def folded(i, u):
-        left = sums[i * domain_len + 2 * u]
-        right = sums[i * domain_len + 2 * u + 1]
-        return jnp.where(low, left + pltpu.roll(left, BLOCK, 1), right + pltpu.roll(right, BLOCK, 1))
-
+    fold(slab, domain_len, aux_id, lambda k: sums[slab * domain_len + k], prior_keep, prior_send)
+    fold(slab, domain_len, aux_id, lambda k: sums[k], own_keep, own_send)
+
+
+def fold(slab, domain_len, aux_id, read, keep, send):
+    half = slab // 2
     for r in range(slab):
-        target = lax.bitwise_xor(aux_id, r)
-        for first, out in ((0, own), (slab, prior)):
-            for u in range(domain_len // 2):
-                out[r, :, u * LANES:(u + 1) * LANES] = folded(first + target, u)
+        first = lax.bitwise_xor(aux_id, r) * domain_len
+        out = keep if r < half else send
+        for u in range(domain_len // 2):
+            left, right = read(first + 2 * u), read(first + 2 * u + 1)
+            low = lax.broadcasted_iota(jnp.int32, left.shape, 1) < BLOCK
+            out[r % half, :, u * LANES:(u + 1) * LANES] = (
+                jnp.where(low, left, right) + pltpu.roll(jnp.where(low, right, left), BLOCK, 1)).astype(out.dtype)
 
 
 def half_blocks(tile_values, tile_pairs, tile_counts, coeffs, domains, slab, pair_size):
@@ -180,13 +183,15 @@
     own_blocks = coeffs.shape[0] // BLOCK
     hits_rows = (2 * slab + 8) // 8 * 8
     sizes = (slots, aux_dev, slab, domain_len, own_blocks, pair_size)
-    out = jax.ShapeDtypeStruct((slab, aux_dev, domain_len * BLOCK), jnp.float32)
+    out = jax.ShapeDtypeStruct((slab // 2, aux_dev, domain_len * BLOCK), jnp.float32)
+    thin = jax.ShapeDtypeStruct(out.shape, jnp.bfloat16)
+    vmem_spec = pl.BlockSpec(memory_space=pltpu.VMEM)
     any_spec = pl.BlockSpec(memory_space=pltpu.HBM)
     return pl.pallas_call(
         functools.partial(half_kernel, sizes),
-        out_shape=[out] * 2,
+        out_shape=[out, thin, thin, thin],
         in_specs=[pl.BlockSpec(memory_space=pltpu.SMEM)] + [any_spec] * 4,
-        out_specs=[pl.BlockSpec(memory_space=pltpu.VMEM)] * 2,
+        out_specs=[vmem_spec] * 4,
         scratch_shapes=[
             pltpu.VMEM((2, slots), jnp.int32),
             pltpu.SMEM((domain_len, orbitals), jnp.int32),
@@ -203,7 +208,7 @@
             pltpu.VMEM((2 * slab * domain_len + 1, aux_dev, LANES), jnp.float32),
             pltpu.SemaphoreType.DMA((5,)),
         ],
-        compiler_params=pltpu.CompilerParams(vmem_limit_bytes=32 * 1024 * 1024),
+        compiler_params=pltpu.CompilerParams(vmem_limit_bytes=16 * 1024 * 1024),
     )(tile_counts, *[pltpu.with_memory_space_constraint(value, pltpu.HBM)
                      for value in (tile_pairs.T, domains.T, coeffs.T, tile_values)])
 
@@ -235,11 +240,16 @@
     aux_size = lax.axis_size("aux")
     slab = coeffs.shape[1] // pair_size
     aux_dev = tile_values.shape[1]
-    own, prior = half_blocks(tile_values, tile_pairs, tile_counts, coeffs, domains, slab, pair_size)
-    blocks = (own + moved(prior, 0, -1)).astype(jnp.bfloat16)
-
-    items = [(blocks, 0, 0)]
-    half = aux_size
+    own_keep, own_send, prior_keep, prior_send = half_blocks(tile_values, tile_pairs, tile_counts, coeffs, domains, slab, pair_size)
+
+    half = aux_size // 2
+    mask = half | 1
+    prior_here = moved(prior_keep, 0, -1)
+    prior_there = moved(prior_send, mask, -1)
+    own_there = moved(own_send, mask, 0)
+    prior_there, prior_here = lax.optimization_barrier((prior_there, prior_here))
+    items = [((prior_here.astype(jnp.float32) + own_keep).astype(jnp.bfloat16), 0, 0),
+             ((prior_there.astype(jnp.float32) + own_there.astype(jnp.float32)).astype(jnp.bfloat16), 1, mask)]
     while half > 2:
         half //= 2
         mask = half | 1
@@ -259,7 +269,7 @@
         in_specs=[pl.BlockSpec(memory_space=pltpu.VMEM)] * (len(arrays) + 1),
         out_specs=pl.BlockSpec(memory_space=pltpu.VMEM),
         scratch_shapes=[pltpu.VMEM((aux_size * aux_dev, virtual.shape[1]), jnp.float32)],
-        compiler_params=pltpu.CompilerParams(vmem_limit_bytes=16 * 1024 * 1024),
+        compiler_params=pltpu.CompilerParams(vmem_limit_bytes=4 * 1024 * 1024),
     )(*arrays, virtual)
 
 

time: 15.5 us -> 14.8 us (0.955)
  waiting for transfers between devices: 6.19 us -> 3.42 us
  starting transfers between devices: 4.63 us -> 7.13 us
  Pallas kernels: 3.77 us -> 3.42 us
    ppermute x3 -> x4, waiting for transfers between devices: 6.19 us -> 3.42 us  [moved(): return lax.ppermute(value, ('aux', 'pair'), routes)]
    ppermute x3 -> x4, starting transfers between devices: 4.63 us -> 7.13 us  [moved(): return lax.ppermute(value, ('aux', 'pair'), routes)]
    pallas_call x1, Pallas kernels: 3.01 us -> 2.66 us  [half_blocks(): pl.pallas_call(functools.partial(half_kernel, sizes), out_shape=[out, thi...]
  transfers between devices with their start and end apart: 3 -> 4, of which waited for: 3 -> 3; matrix products, arithmetic and copies ran while one was open for 0% -> 0% of each run, Pallas kernels for 0% -> 0%
where the time goes in v1:
time: 14.8 us; the launch traced here: 14.7 us
  starting transfers between devices  7.13 us (48%)
  Pallas kernels  3.42 us (23%)
  waiting for transfers between devices  3.42 us (23%)
  between operations  0.73 us (5%)
    ppermute x4, starting transfers between devices, moved(): return lax.ppermute(value, ('aux', 'pair'), routes)  7.13 us
    ppermute x4, waiting for transfers between devices, moved(): return lax.ppermute(value, ('aux', 'pair'), routes)  3.42 us
    pallas_call x1, Pallas kernels, half_blocks(): pl.pallas_call(functools.partial(half_kernel, sizes), out_shape=[out, thi...  2.66 us
    pallas_call x1, Pallas kernels, body(): pl.pallas_call(functools.partial(fit_kernel, sources), out_shape=jax.Shap...  0.76 us
  transfers between devices with their start and end apart: 4, of which 3 were waited for; matrix products, arithmetic and copies ran while one was open for 0% of the time, Pallas kernels for 0%

profile of v1, /device:TPU:0, one launch (start us, length us, event | category | flops | bytes accessed | tf_op | source)
XLA Modules:
  0.0 14.7 jit_solution(15387210576116630527)
XLA Ops:
  0.0 0.0 copy-start
  0.7 2.7 %shard_map.64 = (f32[2,8,512]{2,1,0:T(8,128)S(1)}, bf16[2,8,512]{2,1,0:T(8,128)(2,1)S(1)}, bf16[2,8,512]{2,1,0:T(8,128)(2,1)S(1)}, bf16[2,8,512]{2,1,0:T(8,128)(2,1)S(1)}) custom-call(s32[1]{0:T(128)S(6)} %copy.7.count_s, s32[2,64]{1,0:T(2,128)} %bitcast.5, s32[8,16]{1,0:T(8,128)} %bitcast.4, bf16[16,5120]{1,0:T(8,128)(2,1)} %bitcast.3, ...), custom_call_target="tpu_custom_call" | custom-call | tf_op jit(solution)/shard_map/pallas_call | solution.py:190
  3.4 5.1 %collective-permute-start = (bf16[2,8,512]{2,1,0:T(8,128)(2,1)S(1)}, bf16[2,8,512]{2,1,0:T(8,128)(2,1)S(1)}, u32[]{:S(2)}, u32[]{:S(2)}) collective-permute-start(bf16[2,8,512]{2,1,0:T(8,128)(2,1)S(1)} %get-tuple-element.11), channel_id=1, source_target_pairs={{0,15},{1,12},{2,13},{3,14},{4,11},{5,8},{6,9},{7,10},{8,7},{9,4},... | collective-permute-start | bytes 49160 | tf_op jit(solution)/shard_map/ppermute | solution.py:223
  8.4 1.0 %collective-permute-start.1 = (bf16[2,8,512]{2,1,0:T(8,128)(2,1)S(1)}, bf16[2,8,512]{2,1,0:T(8,128)(2,1)S(1)}, u32[]{:S(2)}, u32[]{:S(2)}) collective-permute-start(bf16[2,8,512]{2,1,0:T(8,128)(2,1)S(1)} %get-tuple-element.12), channel_id=1, source_target_pairs={{0,3},{1,0},{2,1},{3,2},{4,7},{5,4},{6,5},{7,6},{8,11},{9,8},{10,9... | collective-permute-start | bytes 49160 | tf_op jit(solution)/shard_map/ppermute | solution.py:223
  9.4 0.6 %collective-permute-start.2 = (bf16[2,8,512]{2,1,0:T(8,128)(2,1)S(1)}, bf16[2,8,512]{2,1,0:T(8,128)(2,1)S(1)}, u32[]{:S(2)}, u32[]{:S(2)}) collective-permute-start(bf16[2,8,512]{2,1,0:T(8,128)(2,1)S(1)} %get-tuple-element.16), channel_id=1, source_target_pairs={{0,12},{1,13},{2,14},{3,15},{4,8},{5,9},{6,10},{7,11},{8,4},{9,5},... | collective-permute-start | bytes 49160 | tf_op jit(solution)/shard_map/ppermute | solution.py:223
  10.0 0.0 collective-permute-done
  10.0 2.2 %collective-permute-done.1 = bf16[2,8,512]{2,1,0:T(8,128)(2,1)S(1)} collective-permute-done((bf16[2,8,512]{2,1,0:T(8,128)(2,1)S(1)}, bf16[2,8,512]{2,1,0:T(8,128)(2,1)S(1)}, u32[]{:S(2)}, u32[]{:S(2)}) %collective-permute-start.1) | collective-permute-done | bytes 16416 | tf_op jit(solution)/shard_map/ppermute | solution.py:223
  12.2 0.4 %collective-permute-done.2 = bf16[2,8,512]{2,1,0:T(8,128)(2,1)S(1)} collective-permute-done((bf16[2,8,512]{2,1,0:T(8,128)(2,1)S(1)}, bf16[2,8,512]{2,1,0:T(8,128)(2,1)S(1)}, u32[]{:S(2)}, u32[]{:S(2)}) %collective-permute-start.2) | collective-permute-done | bytes 16416 | tf_op jit(solution)/shard_map/ppermute | solution.py:223
  12.6 0.5 %collective-permute-start.3 = (bf16[2,8,512]{2,1,0:T(8,128)(2,1)S(1)}, bf16[2,8,512]{2,1,0:T(8,128)(2,1)S(1)}, u32[]{:S(2)}, u32[]{:S(2)}) collective-permute-start(bf16[2,8,512]{2,1,0:T(8,128)(2,1)S(1)} %pad_maximum_fusion), channel_id=1, source_target_pairs={{0,4},{1,5},{2,6},{3,7},{4,0},{5,1},{6,2},{7,3},{8,12},{9,13},{10,... | collective-permute-start | bytes 49160 | tf_op jit(solution)/shard_map/ppermute | solution.py:223
  13.1 0.8 %collective-permute-done.3.refs_2_ = bf16[2,8,512]{2,1,0:T(8,128)(2,1)S(1)} collective-permute-done((bf16[2,8,512]{2,1,0:T(8,128)(2,1)S(1)}, bf16[2,8,512]{2,1,0:T(8,128)(2,1)S(1)}, u32[]{:S(2)}, u32[]{:S(2)}) %collective-permute-start.3) | collective-permute-done | bytes 16416 | tf_op jit(solution)/shard_map/ppermute | solution.py:223
  14.0 0.0 copy-done
  14.0 0.8 %shard_map.65 = bf16[1,32,256]{2,1,0:T(8,128)(2,1)} custom-call(bf16[2,8,512]{2,1,0:T(8,128)(2,1)S(1)} %add_convert_fusion.1.refs_0_, bf16[2,8,512]{2,1,0:T(8,128)(2,1)S(1)} %add_convert_fusion.refs_1_, bf16[2,8,512]{2,1,0:T(8,128)(2,1)S(1)} %collective-permute-done.3.refs_2_, bf16[1,512,256]{2,1,0:T(8,128)(2,1)S(1)} %copy-done), custom_call_target="tpu_custom_call" | custom-call | tf_op jit(solution)/shard_map/pallas_call | solution.py:266
  (5 shorter events, 0.0 us)
Async XLA Ops:
  0.0 14.0 %copy-start = (bf16[1,512,256]{2,1,0:T(8,128)(2,1)S(1)}, bf16[1,512,256]{2,1,0:T(8,128)(2,1)}, u32[]{:S(2)}) copy-start(bf16[1,512,256]{2,1,0:T(8,128)(2,1)} %refs_3_.1) | copy-start | bytes 786436
  3.4 6.6 %collective-permute-start = (bf16[2,8,512]{2,1,0:T(8,128)(2,1)S(1)}, bf16[2,8,512]{2,1,0:T(8,128)(2,1)S(1)}, u32[]{:S(2)}, u32[]{:S(2)}) collective-permute-start(bf16[2,8,512]{2,1,0:T(8,128)(2,1)S(1)} %get-tuple-element.11), channel_id=1, source_target_pairs={{0,15},{1,12},{2,13},{3,14},{4,11},{5,8},{6,9},{7,10},{8,7},{9,4},... | collective-permute-start | bytes 49160 | tf_op jit(solution)/shard_map/ppermute | solution.py:223
  8.4 3.7 %collective-permute-start.1 = (bf16[2,8,512]{2,1,0:T(8,128)(2,1)S(1)}, bf16[2,8,512]{2,1,0:T(8,128)(2,1)S(1)}, u32[]{:S(2)}, u32[]{:S(2)}) collective-permute-start(bf16[2,8,512]{2,1,0:T(8,128)(2,1)S(1)} %get-tuple-element.12), channel_id=1, source_target_pairs={{0,3},{1,0},{2,1},{3,2},{4,7},{5,4},{6,5},{7,6},{8,11},{9,8},{10,9... | collective-permute-start | bytes 49160 | tf_op jit(solution)/shard_map/ppermute | solution.py:223
  9.4 3.2 %collective-permute-start.2 = (bf16[2,8,512]{2,1,0:T(8,128)(2,1)S(1)}, bf16[2,8,512]{2,1,0:T(8,128)(2,1)S(1)}, u32[]{:S(2)}, u32[]{:S(2)}) collective-permute-start(bf16[2,8,512]{2,1,0:T(8,128)(2,1)S(1)} %get-tuple-element.16), channel_id=1, source_target_pairs={{0,12},{1,13},{2,14},{3,15},{4,8},{5,9},{6,10},{7,11},{8,4},{9,5},... | collective-permute-start | bytes 49160 | tf_op jit(solution)/shard_map/ppermute | solution.py:223
  12.6 1.3 %collective-permute-start.3 = (bf16[2,8,512]{2,1,0:T(8,128)(2,1)S(1)}, bf16[2,8,512]{2,1,0:T(8,128)(2,1)S(1)}, u32[]{:S(2)}, u32[]{:S(2)}) collective-permute-start(bf16[2,8,512]{2,1,0:T(8,128)(2,1)S(1)} %pad_maximum_fusion), channel_id=1, source_target_pairs={{0,4},{1,5},{2,6},{3,7},{4,0},{5,1},{6,2},{7,3},{8,12},{9,13},{10,... | collective-permute-start | bytes 49160 | tf_op jit(solution)/shard_map/ppermute | solution.py:223
